TPU v7x, 1024 devices: a whole 8x8x8 slice. The times are simulated.
1024 devices in a mesh: row: 32 (over z, y_lo), col: 32 (over x, y_hi, core).
Axes of the slice: x: 8, y: 8 (y_hi: 2, y_lo: 4; y = y_hi * 4 + y_lo), z: 8, core: 2. Of those that a mesh axis runs over, the one named last changes fastest.
Arguments:
- basis_vectors: float32 [8, 1048576], P(None, ('row', 'col')), may hold values from -6 to 6
- ham_tiles: float32 [32, 32, 1024, 256], P('row', 'col'), may hold values from -0.1875 to 0.1875
- tile_rows: int32 [32, 32, 4], P('row', 'col'), may hold values from 0 to 127
- tile_cols: int32 [32, 32, 4], P('row', 'col'), may hold values from 0 to 127
- tile_count: int32 [32, 32], P('row', 'col'), may hold values from 1 to 4, as said below
Outputs:
- applied: float32 [8, 1048576], P(None, ('row', 'col'))
Inputs may be any that keep to these rules, and one draw needn't show every extreme that they name: tile_count reaches 4 on some device and 1 on another.
All inputs are finite; a program needn't handle non-finite values.
Results may differ from a plain program's by a relative error of at most 0.0003.
Values sent between devices are 32-bit elements; how exact they have to be, the bound alone decides.
A program may use at most 32 MiB of HBM per device.

v0:
```python
import jax
import jax.numpy as jnp
from jax import lax
from jax.sharding import PartitionSpec as P


def per_device(basis_vectors, ham_tiles, tile_rows, tile_cols, tile_count):
    tile_width = ham_tiles.shape[-1]
    slot_total = ham_tiles.shape[2] // tile_width
    vector_total = basis_vectors.shape[0]
    piece_width = basis_vectors.shape[1]
    row_segment = lax.all_gather(basis_vectors, "col", axis=1, tiled=True)
    col_segment = lax.all_gather(basis_vectors, "row", axis=1, tiled=True)
    all_tiles = ham_tiles.reshape(slot_total, tile_width, tile_width)
    row_tiles = tile_rows.reshape(slot_total)
    col_tiles = tile_cols.reshape(slot_total)
    live_count = tile_count.reshape(())

    def add_slot(slot_index, stacks):
        direct_stack, mirror_stack = stacks
        is_live = (slot_index < live_count).astype(jnp.float32)
        one_tile = lax.dynamic_index_in_dim(all_tiles, slot_index, 0, keepdims=False) * is_live
        row_first = row_tiles[slot_index] * tile_width
        col_first = col_tiles[slot_index] * tile_width
        col_part = lax.dynamic_slice_in_dim(col_segment, col_first, tile_width, 1)
        product_term = lax.dot_general(
            col_part,
            one_tile,
            (((1,), (1,)), ((), ())),
            precision=lax.Precision.HIGHEST,
            preferred_element_type=jnp.float32,
        )
        direct_stack = lax.dynamic_update_index_in_dim(direct_stack, product_term, slot_index, 0)
        row_part = lax.dynamic_slice_in_dim(row_segment, row_first, tile_width, 1)
        product_term = jnp.dot(
            row_part, one_tile, precision=lax.Precision.HIGHEST, preferred_element_type=jnp.float32
        )
        mirror_stack = lax.dynamic_update_index_in_dim(mirror_stack, product_term, slot_index, 0)
        return (direct_stack, mirror_stack)

    empty_stack = jnp.zeros((slot_total, vector_total, tile_width), jnp.float32)
    initial = (empty_stack, empty_stack)

    def one_step(slot_index, stacks):
        return add_slot(slot_index, stacks)

    direct_stack, mirror_stack = lax.fori_loop(0, slot_total, one_step, initial)
    blocks_per_piece = piece_width // tile_width
    block_range = jnp.arange(blocks_per_piece, dtype=jnp.int32)
    row_places = (row_tiles * tile_width).astype(jnp.float32)
    col_places = (col_tiles * tile_width).astype(jnp.float32)

    def make_folder(own_index, received):
        stacked, places = received
        local_block = places.astype(jnp.int32) // tile_width - own_index * blocks_per_piece
        onehot = (local_block[:, None] == block_range[None, :]).astype(jnp.float32)
        return jnp.einsum("sq,svb->vqb", onehot, stacked, precision=lax.Precision.HIGHEST)

    direct_share = make_folder(
        lax.axis_index("col"),
        (
            lax.all_gather(direct_stack, "col", axis=0, tiled=True),
            lax.all_gather(row_places, "col", axis=0, tiled=True),
        ),
    ).reshape(vector_total, piece_width)
    mirror_share = make_folder(
        lax.axis_index("row"),
        (
            lax.all_gather(mirror_stack, "row", axis=0, tiled=True),
            lax.all_gather(col_places, "row", axis=0, tiled=True),
        ),
    ).reshape(vector_total, piece_width)
    return direct_share + mirror_share


def solution(mesh):
    placed = (
        P(None, ("row", "col")),
        P("row", "col", None, None),
        P("row", "col", None),
        P("row", "col", None),
        P("row", "col"),
    )
    return jax.shard_map(
        per_device, mesh=mesh, in_specs=placed, out_specs=P(None, ("row", "col")), check_vma=False
    )
```

profile of v0, /device:TPU:4, one launch (start us, length us, event | category | flops | bytes accessed | tf_op | source)
XLA Modules:
  0.0 558.0 jit_solution(1758383043784341493)
XLA Ops:
  6.5 0.7 all-gather.5.cloned.1.call-update
  7.3 0.7 all-gather.7.cloned.1.call-update
  8.1 170.8 %all-gather.5.cloned.1.call-done = f32[8,32768]{1,0:T(8,128)} async-done(((f32[8,1024]{1,0:T(8,128)}), f32[8,32768]{1,0:T(8,128)}) %all-gather.5.cloned.1.call-update) | async-done | bytes 1048592 | tf_op jit(solution)/shard_map/all_gather | solution.py:13
  178.9 95.6 %all-gather.7.cloned.1.call-done = f32[8,32768]{1,0:T(8,128)} async-done(((f32[8,1024]{1,0:T(8,128)}), f32[8,32768]{1,0:T(8,128)}) %all-gather.7.cloned.1.call-update) | async-done | bytes 1048592 | tf_op jit(solution)/shard_map/all_gather | solution.py:12
  274.5 0.7 copy-done
  275.1 28.1 %while.15 = (s32[]{:T(128)}, f32[4,8,256]{2,1,0:T(8,128)}, f32[4,8,256]{2,1,0:T(8,128)}, s32[4]{0:T(128)S(1)}, f32[8,32768]{1,0:T(8,128)}, /*index=5*/f32[4,256,...) while((s32[]{:T(128)}, f32[4,8,256]{2,1,0:T(8,128)}, ...), condition=%wide.region_1.2_spmd, body=%wide.region_0.1_spmd.sunk | while | flops 12713996 | bytes 561415 | solution.py:47
  275.8 0.7 dynamic_slice.57
  277.1 1.9 fusion.32
  279.0 0.6 dynamic_slice.58
  280.3 1.8 fusion.33
  282.8 0.7 dynamic_slice.57
  284.1 1.9 fusion.32
  286.0 0.6 dynamic_slice.58
  287.4 1.8 fusion.33
  289.8 0.7 dynamic_slice.57
  291.2 1.9 fusion.32
  293.1 0.6 dynamic_slice.58
  294.4 1.8 fusion.33
  296.9 0.7 dynamic_slice.57
  298.2 1.9 fusion.32
  300.1 0.6 dynamic_slice.58
  301.4 1.8 fusion.33
  303.3 0.5 all-gather.11.cloned.1.call-update
  303.9 1.2 dynamic-slice
  305.1 1.3 dynamic-slice.1
  307.7 0.1 convert_dynamic-update-slice_fusion.1
  307.8 74.9 %all-reduce = f32[128]{0:T(128)S(1)} all-reduce(f32[128]{0:T(128)S(1)} %convert_dynamic-update-slice_fusion.1), channel_id=1, replica_groups=mesh['row'=32,'col'=32] {'col'}, use_global_device_ids=true, to_apply=%add | all-reduce | flops 128 | bytes 1024
  382.8 81.2 %all-reduce.1 = f32[128]{0:T(128)S(1)} all-reduce(f32[128]{0:T(128)S(1)} %convert_dynamic-update-slice_fusion), channel_id=1, replica_groups=mesh['row'=32,'col'=32] {'row'}, use_global_device_ids=true, to_apply=%add.1 | all-reduce | flops 128 | bytes 1024
  464.0 1.9 fusion.12
  465.9 83.0 %all-gather.11.cloned.1.call-done = f32[128,8,256]{2,1,0:T(8,128)} async-done(((f32[4,8,256]{2,1,0:T(8,128)}), f32[128,8,256]{2,1,0:T(8,128)}) %all-gather.11.cloned.1.call-update) | async-done | bytes 1048592 | tf_op jit(solution)/shard_map/all_gather | solution.py:69
  549.0 1.9 fusion.10
  550.9 0.6 copy.10
  (16 shorter events, 0.3 us)
Async XLA Ops:
  6.5 172.3 %all-gather.5.cloned.1.call-start = ((), (), s32[]{:S(2)}) async-start(), calls=%async_computation | async-start | bytes 1081344 | tf_op jit(solution)/shard_map/all_gather | solution.py:13
  7.3 267.2 %all-gather.7.cloned.1.call-start = ((), (), s32[]{:S(2)}) async-start(), calls=%async_computation.1 | async-start | bytes 1081344 | tf_op jit(solution)/shard_map/all_gather | solution.py:12
  8.0 456.0 %all-gather.9.cloned.1.call-start = ((), (), s32[]{:S(2)}) async-start(), calls=%async_computation.2 | async-start | bytes 1081344 | tf_op jit(solution)/shard_map/all_gather | solution.py:62
  274.4 0.7 copy-start
  274.5 0.7 copy-start.1
  303.3 245.7 %all-gather.11.cloned.1.call-start = ((), (), s32[]{:S(2)}) async-start(), calls=%async_computation.3 | async-start | bytes 1081344 | tf_op jit(solution)/shard_map/all_gather | solution.py:69
Sparse Core Ops, SparseCore 0:
  10.0 168.8 all-gather.4
  183.4 91.0 all-gather.6
  303.4 88.9 all-gather.8
  394.9 154.0 all-gather.10
where the time goes:
time: 559 us; the launch traced here: 558 us
  waiting for transfers between devices  351 us (63%)
  blocking collectives  156 us (28%)
  matrix products  18.7 us (3%)
  between operations  14.4 us (3%)
  local copies, waits for them, and re-layouts  9.08 us (2%)
  loops' own time  8.11 us (1%)
    all_gather x1, waiting for transfers between devices, per_device(): col_segment = lax.all_gather(basis_vectors, 'row', axis=1, tiled=True)  171 us
    unnamed x2, blocking collectives  156 us
    all_gather x1, waiting for transfers between devices, per_device(): row_segment = lax.all_gather(basis_vectors, 'col', axis=1, tiled=True)  95.6 us
    all_gather x1, waiting for transfers between devices, per_device(): lax.all_gather(mirror_stack, 'row', axis=0, tiled=True)  83 us
  transfers between devices with their start and end apart: 4, of which 3 were waited for; matrix products, arithmetic and copies ran while one was open for 1% of the time, Pallas kernels for 0%

commit v1 on v0

v1 whole, which is shorter than its diff:
```python
import functools

import jax
import jax.numpy as jnp
from jax import lax
from jax.experimental import pallas as pl
from jax.experimental.pallas import tpu as pltpu
from jax.sharding import PartitionSpec as P

MESH = pl.DeviceIdType.MESH
AXES = ("col", "row")
SMALL = 4


def kernel(
    bigs,
    subs,
    vectors_hbm,
    tiles_hbm,
    rows_hbm,
    cols_hbm,
    count_hbm,
    out_ref,
    tiles,
    high,
    low,
    vectors,
    own,
    given_rows,
    given_cols,
    given_count,
    places,
    held_0,
    held_1,
    stage,
    picked_0,
    picked_1,
    products,
    marks,
    partial,
    arrived,
    ready,
    local_sem,
    place_send,
    place_recv,
    wide_send,
    wide_recv,
    pick_send,
    pick_recv,
    product_send,
    product_recv,
    sum_send,
    sum_recv,
):
    slots, width = tiles.shape[0], tiles.shape[1]
    small = SMALL
    given = (given_rows, given_cols)
    held, picked = (held_0, held_1), (picked_0, picked_1)
    me = [lax.axis_index(axis) for axis in AXES]
    my_big = [lax.div(m, small) for m in me]
    my_small = [lax.rem(m, small) for m in me]

    def each_big(a, act):
        @pl.loop(0, bigs[a])
        def _(rank):
            big = rank
            if a == 0:
                odd = lax.rem(rank, 2)
                half = lax.div(rank + 1, 2)
                big = odd * half + (1 - odd) * lax.rem(bigs[a] - half, bigs[a])

            @pl.when(big != my_big[a])
            def _():
                act(big)

    def each_small(a, act):
        @pl.loop(1, small)
        def _(step):
            act(lax.rem(my_small[a] + step, small))

    def at(a, big, little):
        return {AXES[a]: big * small + little}

    core = lax.rem(me[0], 2)
    first_core = core == 0
    barrier = pltpu.get_barrier_semaphore()

    def greet(**where):
        pl.semaphore_signal(barrier, inc=1, device_id=where, device_id_type=MESH)

    each_big(0, lambda big: greet(col=big * small + my_small[0] - core))

    @pl.loop(1, small // 2)
    def _(step):
        greet(col=my_big[0] * small + lax.rem(my_small[0] - core + 2 * step, small))

    @pl.when(core == 1)
    def _():
        greet(col=me[0] - 1)

    each_big(1, lambda big: greet(row=big * small + my_small[1], col=me[0] - core + 1))
    each_small(
        1, lambda little: greet(row=my_big[1] * small + little, col=me[0] - core + 1)
    )

    local = [
        pltpu.make_async_copy(source, target, local_sem.at[index])
        for index, (source, target) in enumerate(
            [
                (vectors_hbm, vectors),
                (rows_hbm, given_rows),
                (cols_hbm, given_cols),
                (count_hbm, given_count),
                (tiles_hbm, tiles),
            ]
        )
    ]
    for copy in local:
        copy.start()
    for copy in local[:-1]:
        copy.wait()

    for sub in range(subs):
        own[sub] = vectors[:, sub * width : (sub + 1) * width]
    for a in range(2):
        for slot in range(slots):
            place = given[a][0, 0, slot]
            places[a, my_small[a], slot] = place
            places[a, my_small[a], slots + slot] = lax.div(place, small * subs) * subs + lax.rem(
                place, subs
            )

    def complete(a):
        mine = first_core if a == 0 else core == 1
        count = 2 * (bigs[0] - 1) + small - 1 if a == 0 else 2 * (bigs[1] + small - 2)

        @pl.when(mine)
        def _():
            pl.semaphore_wait(barrier, count)
            pl.semaphore_signal(
                ready, inc=1, device_id={"col": me[0] + 1 - 2 * a}, device_id_type=MESH
            )

        @pl.when(jnp.logical_not(mine))
        def _():
            pl.semaphore_wait(ready, 1)

    def place_copy(a, little):
        mine = places.at[a, my_small[a]]
        return pltpu.make_async_remote_copy(
            src_ref=mine,
            dst_ref=mine,
            send_sem=place_send.at[a],
            recv_sem=place_recv.at[a],
            device_id=at(a, my_big[a], little),
            device_id_type=MESH,
        )

    def wide_copy(a, big):
        return pltpu.make_async_remote_copy(
            src_ref=own,
            dst_ref=held[a].at[pl.ds(my_big[a] * subs, subs)],
            send_sem=wide_send.at[a],
            recv_sem=wide_recv.at[a],
            device_id=at(a, big, my_small[a]),
            device_id_type=MESH,
        )

    for a in range(2):
        complete(a)
        each_big(a, lambda big: wide_copy(a, big).start())
        each_small(a, lambda little: place_copy(a, little).start())
    for a in range(2):
        for sub in range(subs):
            held[a][my_big[a] * subs + sub] = own[sub]

    local[-1].wait()
    for slot in range(slots):
        whole = tiles[slot]
        top = whole.astype(jnp.bfloat16)
        high[slot] = top
        low[slot] = (whole - top.astype(jnp.float32)).astype(jnp.bfloat16)

    def wait_all(buffer, count, sem):
        landed = buffer.at[pl.ds(0, count)]
        pltpu.make_async_copy(landed, landed, sem).wait()

    def pick_copy(a, step):
        return pltpu.make_async_remote_copy(
            src_ref=stage.at[a, step],
            dst_ref=picked[a].at[pl.ds(my_small[a] * slots, slots)],
            send_sem=pick_send.at[a],
            recv_sem=pick_recv.at[a],
            device_id=at(a, my_big[a], lax.rem(my_small[a] + step, small)),
            device_id_type=MESH,
        )

    def pick(a):
        wait_all(held[a], (bigs[a] - 1) * subs, wide_recv.at[a])
        for step in range(1, small):
            little = lax.rem(my_small[a] + step, small)
            for slot in range(slots):
                stage[a, step, slot] = held[a][places[a, little, slots + slot]]
            pick_copy(a, step).start()
        for slot in range(slots):
            picked[a][my_small[a] * slots + slot] = held[a][places[a, my_small[a], slots + slot]]

    def mark(a):
        for index in range(small * slots):
            marks[a, index] = jnp.full(
                marks.shape[2:], places[a, index // slots, index % slots], jnp.int32
            )

    def block(a, slot):
        place = given[a][0, 0, slot]
        return picked[a][lax.rem(lax.div(place, subs), small) * slots + slot]

    def multiply(value, slot, tile_dim):
        top = value.astype(jnp.bfloat16).astype(jnp.float32)
        both = jnp.concatenate([top, value - top], axis=0).astype(jnp.bfloat16)
        dims = (((1,), (tile_dim,)), ((), ()))
        result = lax.dot_general(both, high[slot], dims, preferred_element_type=jnp.float32)
        result += lax.dot_general(both, low[slot], dims, preferred_element_type=jnp.float32)
        return result[: value.shape[0]] + result[value.shape[0] :]

    def product_copy(a, little):
        mine = products.at[a, pl.ds(my_small[a] * slots, slots)]
        return pltpu.make_async_remote_copy(
            src_ref=mine,
            dst_ref=mine,
            send_sem=product_send.at[a],
            recv_sem=product_recv.at[a],
            device_id=at(a, my_big[a], little),
            device_id_type=MESH,
        )

    def apply_tiles(a):
        wait_all(picked[1 - a], (small - 1) * slots, pick_recv.at[1 - a])
        for slot in range(slots):
            is_live = (slot < given_count[0, 0]).astype(jnp.float32)
            products[a, my_small[a] * slots + slot] = is_live * multiply(block(1 - a, slot), slot, 1 - a)
        each_small(a, lambda little: product_copy(a, little).start())

    def sum_copy(a, big):
        return pltpu.make_async_remote_copy(
            src_ref=partial.at[a, big],
            dst_ref=arrived.at[a, my_big[a]],
            send_sem=sum_send.at[a],
            recv_sem=sum_recv.at[a],
            device_id=at(a, big, my_small[a]),
            device_id_type=MESH,
        )

    def sum_for(a, big, target, target_index):
        first = (big * small + my_small[a]) * subs
        totals = [jnp.zeros(products.shape[2:], jnp.float32) for _ in range(subs)]
        for index in range(small * slots):
            value = products[a, index]
            spread = jnp.concatenate([marks[a, index]] * (width // marks.shape[3]), axis=1)
            for sub in range(subs):
                totals[sub] += jnp.where(spread == first + sub, value, 0.0)
        for sub in range(subs):
            target[a, target_index, sub] = totals[sub]

    def send_sum(a, big):
        sum_for(a, big, partial, big)
        sum_copy(a, big).start()

    def sums(a):
        wait_all(products.at[a], (small - 1) * slots, product_recv.at[a])
        each_big(a, lambda big: send_sum(a, big))
        sum_for(a, my_big[a], arrived, my_big[a])

    for a in range(2):
        wait_all(places.at[a], small - 1, place_recv.at[a])
    pick(0)
    pick(1)
    mark(1)
    apply_tiles(1)
    mark(0)
    apply_tiles(0)
    sums(1)
    sums(0)

    totals = []
    for a in range(2):
        wait_all(arrived.at[a], bigs[a] - 1, sum_recv.at[a])
        for sub in range(subs):
            total = arrived[a, 0, sub]
            for big in range(1, bigs[a]):
                total += arrived[a, big, sub]
            totals.append(total)
    for sub in range(subs):
        out_ref[:, sub * width : (sub + 1) * width] = totals[sub] + totals[subs + sub]

    for a in range(2):
        wait_all(places.at[a], small - 1, place_send.at[a])
        wait_all(held[a], (bigs[a] - 1) * subs, wide_send.at[a])
        wait_all(stage.at[a], small - 1, pick_send.at[a])
        wait_all(products.at[a], (small - 1) * slots, product_send.at[a])
        wait_all(partial.at[a], bigs[a] - 1, sum_send.at[a])


def solution(mesh):
    bigs = tuple(mesh.shape[axis] // SMALL for axis in AXES)
    most = max(bigs)

    def per_device(basis_vectors, ham_tiles, tile_rows, tile_cols, tile_count):
        vecs, piece = basis_vectors.shape
        width = ham_tiles.shape[-1]
        slots = ham_tiles.shape[2] // width
        subs = piece // width
        block = (vecs, width)
        dma = pltpu.SemaphoreType.DMA
        place = pltpu.SMEM((1, 1, slots), jnp.int32)
        return pl.pallas_call(
            functools.partial(kernel, bigs, subs),
            out_shape=pltpu.VMEM((vecs, piece), jnp.float32),
            in_specs=[pl.BlockSpec(memory_space=pl.ANY)] * 5,
            out_specs=pl.BlockSpec(memory_space=pltpu.VMEM),
            scratch_shapes=[
                pltpu.VMEM((slots, width, width), jnp.float32),
                pltpu.VMEM((slots, width, width), jnp.bfloat16),
                pltpu.VMEM((slots, width, width), jnp.bfloat16),
                pltpu.VMEM((vecs, piece), jnp.float32),
                pltpu.VMEM((subs,) + block, jnp.float32),
                place,
                place,
                pltpu.SMEM((1, 1), jnp.int32),
                pltpu.SMEM((2, SMALL, 2 * slots), jnp.int32),
                pltpu.VMEM((bigs[0] * subs,) + block, jnp.float32),
                pltpu.VMEM((bigs[1] * subs,) + block, jnp.float32),
                pltpu.VMEM((2, SMALL, slots) + block, jnp.float32),
                pltpu.VMEM((SMALL * slots,) + block, jnp.float32),
                pltpu.VMEM((SMALL * slots,) + block, jnp.float32),
                pltpu.VMEM((2, SMALL * slots) + block, jnp.float32),
                pltpu.VMEM((2, SMALL * slots, 8, 128), jnp.int32),
                pltpu.VMEM((2, most, subs) + block, jnp.float32),
                pltpu.VMEM((2, most, subs) + block, jnp.float32),
                pltpu.SemaphoreType.REGULAR,
                dma((5,)),
            ]
            + [dma((2,))] * 10,
            compiler_params=pltpu.CompilerParams(collective_id=0, has_side_effects=True),
            name="apply_pairs",
        )(basis_vectors, ham_tiles.reshape(slots, width, width), tile_rows, tile_cols, tile_count)

    placed = (
        P(None, ("row", "col")),
        P("row", "col", None, None),
        P("row", "col", None),
        P("row", "col", None),
        P("row", "col"),
    )
    return jax.shard_map(
        per_device, mesh=mesh, in_specs=placed, out_specs=P(None, ("row", "col")), check_vma=False
    )
```

time: 559 us -> 50.8 us (0.09)
  the two profiles are of different devices: /device:TPU:4 before, /device:TPU:21 now
where the time goes in v1:
time: 50.8 us; the launch traced here: 50.6 us
  Pallas kernels  49.3 us (97%)
  between operations  0.66 us (1%)
  local copies, waits for them, and re-layouts  0.62 us (1%)
    pallas_call x1, Pallas kernels, per_device(): pl.pallas_call(functools.partial(kernel, bigs, subs), out_shape=pltpu.VME...  49.3 us

profile of v1, /device:TPU:21, one launch (start us, length us, event | category | flops | bytes accessed | tf_op | source)
XLA Modules:
  0.0 50.6 jit_solution(18442564042645534912)
XLA Ops:
  0.7 49.3 %apply_pairs.1 = f32[8,1024]{1,0:T(8,128)S(1)} custom-call(f32[8,1024]{1,0:T(8,128)} %vectors_hbm.1, f32[4,256,256]{2,1,0:T(8,128)} %bitcast.1, s32[1,1,4]{2,1,0:T(1,128)} %rows_hbm.1, s32[1,1,4]{2,1,0:T(1,128)} %cols_hbm.1, s32[1,1]{1,0:T(1,128)S(6)} %copy.8.count_hbm), custom_call_target="tpu_custom_call" | custom-call | tf_op jit(solution)/shard_map/apply_pairs/pallas_call | solution.py:316
  50.0 0.6 %copy.7 = f32[8,1024]{1,0:T(8,128)} copy(f32[8,1024]{1,0:T(8,128)S(1)} %apply_pairs.1) | data formatting | bytes 65536

commit v2 on v1

--- a/solution.py
+++ b/solution.py
@@ -60,14 +60,17 @@
     my_big = [lax.div(m, small) for m in me]
     my_small = [lax.rem(m, small) for m in me]
 
-    def each_big(a, act):
+    def each_big(a, act, farthest=False):
         @pl.loop(0, bigs[a])
         def _(rank):
             big = rank
             if a == 0:
-                odd = lax.rem(rank, 2)
                 half = lax.div(rank + 1, 2)
-                big = odd * half + (1 - odd) * lax.rem(bigs[a] - half, bigs[a])
+                offset = (1 - 2 * lax.rem(rank, 2)) * half
+                if farthest:
+                    big = lax.rem(my_big[0] + bigs[0] // 2 + offset + bigs[0], bigs[0])
+                else:
+                    big = lax.rem(bigs[0] - offset, bigs[0])
 
             @pl.when(big != my_big[a])
             def _():
@@ -82,25 +85,32 @@
         return {AXES[a]: big * small + little}
 
     core = lax.rem(me[0], 2)
-    first_core = core == 0
+    first_late = bigs[1] // 2
+    late = my_big[1] >= first_late
+    is_late = late.astype(jnp.int32)
     barrier = pltpu.get_barrier_semaphore()
 
     def greet(**where):
         pl.semaphore_signal(barrier, inc=1, device_id=where, device_id_type=MESH)
 
+    def touches_late(big):
+        return jnp.maximum((big >= first_late).astype(jnp.int32), is_late)
+
     each_big(0, lambda big: greet(col=big * small + my_small[0] - core))
+    each_big(
+        1, lambda big: greet(row=big * small + my_small[1], col=me[0] - core + touches_late(big))
+    )
 
     @pl.loop(1, small // 2)
     def _(step):
         greet(col=my_big[0] * small + lax.rem(my_small[0] - core + 2 * step, small))
 
-    @pl.when(core == 1)
-    def _():
-        greet(col=me[0] - 1)
-
-    each_big(1, lambda big: greet(row=big * small + my_small[1], col=me[0] - core + 1))
-    each_small(
-        1, lambda little: greet(row=my_big[1] * small + little, col=me[0] - core + 1)
+    each_small(1, lambda little: greet(row=my_big[1] * small + little, col=me[0] - core))
+    greet(col=me[0] + 1 - 2 * core)
+    together = (1 - is_late) * (first_late - 1)
+    counts = (
+        2 * (bigs[0] - 1) + (small - 2) + 2 * (small - 1) + 2 * together + 1,
+        2 * (bigs[1] - 1 - together) + 1,
     )
 
     local = [
@@ -130,18 +140,15 @@
                 place, subs
             )
 
-    def complete(a):
-        mine = first_core if a == 0 else core == 1
-        count = 2 * (bigs[0] - 1) + small - 1 if a == 0 else 2 * (bigs[1] + small - 2)
-
-        @pl.when(mine)
+    def complete(gate):
+        @pl.when(core == gate)
         def _():
-            pl.semaphore_wait(barrier, count)
+            pl.semaphore_wait(barrier, counts[gate])
             pl.semaphore_signal(
-                ready, inc=1, device_id={"col": me[0] + 1 - 2 * a}, device_id_type=MESH
+                ready, inc=1, device_id={"col": me[0] + 1 - 2 * gate}, device_id_type=MESH
             )
 
-        @pl.when(jnp.logical_not(mine))
+        @pl.when(core != gate)
         def _():
             pl.semaphore_wait(ready, 1)
 
@@ -166,20 +173,29 @@
             device_id_type=MESH,
         )
 
-    for a in range(2):
-        complete(a)
-        each_big(a, lambda big: wide_copy(a, big).start())
-        each_small(a, lambda little: place_copy(a, little).start())
+    def spread(a, chosen):
+        def one(big):
+            @pl.when(chosen(big))
+            def _():
+                wide_copy(a, big).start()
+
+        each_big(a, one, farthest=True)
+
+    def spread_places():
+        for a in range(2):
+            each_small(a, lambda little: place_copy(a, little).start())
+
     for a in range(2):
         for sub in range(subs):
             held[a][my_big[a] * subs + sub] = own[sub]
 
-    local[-1].wait()
-    for slot in range(slots):
-        whole = tiles[slot]
-        top = whole.astype(jnp.bfloat16)
-        high[slot] = top
-        low[slot] = (whole - top.astype(jnp.float32)).astype(jnp.bfloat16)
+    def split_tiles():
+        local[-1].wait()
+        for slot in range(slots):
+            whole = tiles[slot]
+            top = whole.astype(jnp.bfloat16)
+            high[slot] = top
+            low[slot] = (whole - top.astype(jnp.float32)).astype(jnp.bfloat16)
 
     def wait_all(buffer, count, sem):
         landed = buffer.at[pl.ds(0, count)]
@@ -196,6 +212,7 @@
         )
 
     def pick(a):
+        wait_all(places.at[a], small - 1, place_recv.at[a])
         wait_all(held[a], (bigs[a] - 1) * subs, wide_recv.at[a])
         for step in range(1, small):
             little = lax.rem(my_small[a] + step, small)
@@ -268,19 +285,52 @@
 
     def sums(a):
         wait_all(products.at[a], (small - 1) * slots, product_recv.at[a])
-        each_big(a, lambda big: send_sum(a, big))
+        each_big(a, lambda big: send_sum(a, big), farthest=True)
         sum_for(a, my_big[a], arrived, my_big[a])
 
-    for a in range(2):
-        wait_all(places.at[a], small - 1, place_recv.at[a])
-    pick(0)
-    pick(1)
-    mark(1)
-    apply_tiles(1)
-    mark(0)
-    apply_tiles(0)
-    sums(1)
-    sums(0)
+    def start_first():
+        complete(0)
+        spread(1, lambda big: touches_late(big) == 0)
+        spread(0, lambda big: big >= 0)
+        spread_places()
+
+    def start_second():
+        complete(1)
+        spread(1, lambda big: touches_late(big) == 1)
+
+    @pl.when(late)
+    def _():
+        start_second()
+
+    start_first()
+
+    @pl.when(jnp.logical_not(late))
+    def _():
+        start_second()
+
+    split_tiles()
+
+    @pl.when(jnp.logical_not(late))
+    def _():
+        pick(0)
+        pick(1)
+        apply_tiles(0)
+        apply_tiles(1)
+        mark(0)
+        sums(0)
+        mark(1)
+        sums(1)
+
+    @pl.when(late)
+    def _():
+        pick(0)
+        apply_tiles(1)
+        pick(1)
+        mark(1)
+        sums(1)
+        apply_tiles(0)
+        mark(0)
+        sums(0)
 
     totals = []
     for a in range(2):

time: 50.8 us -> 48.9 us (0.963)
  the two profiles are of different devices: /device:TPU:21 before, /device:TPU:52 now
where the time goes in v2:
time: 48.9 us; the launch traced here: 48.7 us
  Pallas kernels  47.4 us (97%)
  between operations  0.66 us (1%)
  local copies, waits for them, and re-layouts  0.62 us (1%)
    pallas_call x1, Pallas kernels, per_device(): pl.pallas_call(functools.partial(kernel, bigs, subs), out_shape=pltpu.VME...  47.4 us

profile of v2, /device:TPU:52, one launch (start us, length us, event | category | flops | bytes accessed | tf_op | source)
XLA Modules:
  0.0 48.7 jit_solution(2182845360066054301)
XLA Ops:
  0.7 47.4 %apply_pairs.1 = f32[8,1024]{1,0:T(8,128)S(1)} custom-call(f32[8,1024]{1,0:T(8,128)} %vectors_hbm.1, f32[4,256,256]{2,1,0:T(8,128)} %bitcast.1, s32[1,1,4]{2,1,0:T(1,128)} %rows_hbm.1, s32[1,1,4]{2,1,0:T(1,128)} %cols_hbm.1, s32[1,1]{1,0:T(1,128)S(6)} %copy.8.count_hbm), custom_call_target="tpu_custom_call" | custom-call | tf_op jit(solution)/shard_map/apply_pairs/pallas_call | solution.py:366
  48.1 0.6 %copy.7 = f32[8,1024]{1,0:T(8,128)} copy(f32[8,1024]{1,0:T(8,128)S(1)} %apply_pairs.1) | data formatting | bytes 65536

commit v3 on v2

--- a/solution.py
+++ b/solution.py
@@ -76,10 +76,16 @@
             def _():
                 act(big)
 
+    steps = range(small - 1, 0, -1)
+
+    def beside(a, step):
+        if step == 1:
+            return my_small[a] + 1 - 2 * lax.rem(my_small[a], 2)
+        return lax.rem(my_small[a] + 2, 4) if step == 2 else 3 - my_small[a]
+
     def each_small(a, act):
-        @pl.loop(1, small)
-        def _(step):
-            act(lax.rem(my_small[a] + step, small))
+        for step in steps:
+            act(beside(a, step))
 
     def at(a, big, little):
         return {AXES[a]: big * small + little}
@@ -97,16 +103,15 @@
         return jnp.maximum((big >= first_late).astype(jnp.int32), is_late)
 
     each_big(0, lambda big: greet(col=big * small + my_small[0] - core))
+    @pl.loop(1, small // 2)
+    def _(step):
+        greet(col=my_big[0] * small + lax.rem(my_small[0] - core + 2 * step, small))
+
+    each_small(1, lambda little: greet(row=my_big[1] * small + little, col=me[0] - core))
+    greet(col=me[0] + 1 - 2 * core)
     each_big(
         1, lambda big: greet(row=big * small + my_small[1], col=me[0] - core + touches_late(big))
     )
-
-    @pl.loop(1, small // 2)
-    def _(step):
-        greet(col=my_big[0] * small + lax.rem(my_small[0] - core + 2 * step, small))
-
-    each_small(1, lambda little: greet(row=my_big[1] * small + little, col=me[0] - core))
-    greet(col=me[0] + 1 - 2 * core)
     together = (1 - is_late) * (first_late - 1)
     counts = (
         2 * (bigs[0] - 1) + (small - 2) + 2 * (small - 1) + 2 * together + 1,
@@ -207,15 +212,15 @@
             dst_ref=picked[a].at[pl.ds(my_small[a] * slots, slots)],
             send_sem=pick_send.at[a],
             recv_sem=pick_recv.at[a],
-            device_id=at(a, my_big[a], lax.rem(my_small[a] + step, small)),
+            device_id=at(a, my_big[a], beside(a, step)),
             device_id_type=MESH,
         )
 
     def pick(a):
         wait_all(places.at[a], small - 1, place_recv.at[a])
         wait_all(held[a], (bigs[a] - 1) * subs, wide_recv.at[a])
-        for step in range(1, small):
-            little = lax.rem(my_small[a] + step, small)
+        for step in steps:
+            little = beside(a, step)
             for slot in range(slots):
                 stage[a, step, slot] = held[a][places[a, little, slots + slot]]
             pick_copy(a, step).start()
@@ -285,7 +290,7 @@
 
     def sums(a):
         wait_all(products.at[a], (small - 1) * slots, product_recv.at[a])
-        each_big(a, lambda big: send_sum(a, big), farthest=True)
+        each_big(a, lambda big: send_sum(a, big))
         sum_for(a, my_big[a], arrived, my_big[a])
 
     def start_first():
@@ -324,8 +329,8 @@
     @pl.when(late)
     def _():
         pick(0)
+        pick(1)
         apply_tiles(1)
-        pick(1)
         mark(1)
         sums(1)
         apply_tiles(0)

time: 48.9 us -> 48.8 us (level)
  the two profiles are of different devices: /device:TPU:52 before, /device:TPU:2 now
where the time goes in v3:
time: 48.8 us; the launch traced here: 48.7 us
  Pallas kernels  47.4 us (97%)
  between operations  0.66 us (1%)
  local copies, waits for them, and re-layouts  0.62 us (1%)
    pallas_call x1, Pallas kernels, per_device(): pl.pallas_call(functools.partial(kernel, bigs, subs), out_shape=pltpu.VME...  47.4 us

profile of v3, /device:TPU:2, one launch (start us, length us, event | category | flops | bytes accessed | tf_op | source)
XLA Modules:
  0.0 48.7 jit_solution(9471245534046493465)
XLA Ops:
  0.7 47.4 %apply_pairs.1 = f32[8,1024]{1,0:T(8,128)S(1)} custom-call(f32[8,1024]{1,0:T(8,128)} %vectors_hbm.1, f32[4,256,256]{2,1,0:T(8,128)} %bitcast.1, s32[1,1,4]{2,1,0:T(1,128)} %rows_hbm.1, s32[1,1,4]{2,1,0:T(1,128)} %cols_hbm.1, s32[1,1]{1,0:T(1,128)S(6)} %copy.8.count_hbm), custom_call_target="tpu_custom_call" | custom-call | tf_op jit(solution)/shard_map/apply_pairs/pallas_call | solution.py:371
  48.0 0.6 %copy.7 = f32[8,1024]{1,0:T(8,128)} copy(f32[8,1024]{1,0:T(8,128)S(1)} %apply_pairs.1) | data formatting | bytes 65536
